TPU v7x, 128 devices: a whole 4x4x4 slice. The times are simulated.
128 devices in a mesh: depth: 4 (over y), tile: 32 (over z, x, core).
Axes of the slice: x: 4, y: 4, z: 4, core: 2. Of those that a mesh axis runs over, the one named last changes fastest.
Arguments:
- field: float32 [128, 2048, 2048], P('depth', 'tile'), may hold values from -1 to 1
- absorb_coef: float32 [2], replicated, may hold values from 0.01 to 0.04
- color_coef: float32 [3, 4], replicated, may hold values from -1 to 1
- light: float32 [3], replicated, may hold values from -1 to 1
Outputs:
- image: float32 [4, 2048, 2048], P(None, 'tile', 'depth')
All inputs are finite; a program needn't handle non-finite values.
Results may differ from a plain program's by a relative error of at most 0.0003.
Values sent between devices are 32-bit elements; how exact they have to be, the bound alone decides.
A program may use at most 192 MiB of HBM per device.

v0:
```python
import jax
import jax.numpy as jnp
from jax import lax
from jax.sharding import PartitionSpec as P


def with_halo(value, sides, width):
    for axis, dim in sides:
        peers, length = (lax.axis_size(axis), value.shape[dim])
        up = [(i, (i + 1) % peers) for i in range(peers - 1)]
        down = [(j, i) for i, j in up]
        last = lax.slice_in_dim(value, length - width, length, axis=dim)
        initial = lax.slice_in_dim(value, 0, width, axis=dim)
        before = lax.ppermute(last, axis, up)
        after = lax.ppermute(initial, axis, down)
        value = jnp.concatenate([before, value, after], axis=dim)
    return value


def slab_light(padded, absorb_coef, color_coef, light):
    center = padded[1:-1, 1:-1]
    grad_z = 0.5 * (padded[2:, 1:-1] - padded[:-2, 1:-1])
    grad_x = 0.5 * (padded[1:-1, 2:] - padded[1:-1, :-2])
    side_pad = jnp.pad(center, ((0, 0), (0, 0), (1, 1)))
    grad_y = 0.5 * (side_pad[:, :, 2:] - side_pad[:, :, :-2])
    facing = jnp.abs(light[0] * grad_z + light[1] * grad_x + light[2] * grad_y)
    shade = facing / jnp.sqrt(grad_z * grad_z + grad_x * grad_x + grad_y * grad_y + 1.0)
    sigma = absorb_coef[0] + absorb_coef[1] * center * center
    coef = color_coef[:, :, None, None, None]
    poly = coef[:, 0] + center * (coef[:, 1] + center * (coef[:, 2] + center * coef[:, 3]))
    return (sigma, shade[None] * poly)


def over_front(front, back):
    return front + (1.0 - front[3:4]) * back


def on_device(field, absorb_coef, color_coef, light):
    padded = with_halo(field, (("depth", 0), ("tile", 1)), 1)
    sigma, emitted = slab_light(padded, absorb_coef, color_coef, light)
    running = jnp.cumsum(sigma, axis=0)
    before = running - sigma
    weight = (1.0 - jnp.exp(-sigma)) * jnp.exp(-before)
    color = jnp.sum(emitted * weight[None], axis=1)
    optical = running[-1]
    partial_image = jnp.concatenate([color, (1.0 - jnp.exp(-optical))[None]], axis=0)
    pieces = lax.all_to_all(partial_image[None], "depth", split_axis=3, concat_axis=0, tiled=True)
    total = pieces[0]
    for slab in range(1, pieces.shape[0]):
        total = over_front(total, pieces[slab])
    return total


def solution(mesh):
    in_specs = (P("depth", "tile", None), P(), P(), P())
    out_specs = P(None, "tile", "depth")
    return jax.shard_map(
        on_device, mesh=mesh, in_specs=in_specs, out_specs=out_specs, check_vma=False
    )
```

profile of v0, /device:TPU:15, one launch (start us, length us, event | category | flops | bytes accessed | tf_op | source)
XLA Modules:
  0.0 190.1 jit_solution(7068921546794885464)
XLA Ops:
  0.0 1.3 fusion.18
  1.3 3.2 %collective-permute-start.1 = (f32[1,64,2048]{2,1,0:T(8,128)S(1)}, f32[1,64,2048]{2,1,0:T(8,128)S(1)}, u32[]{:S(2)}, u32[]{:S(2)}) collective-permute-start(f32[1,64,2048]{2,1,0:T(8,128)S(1)} %get-tuple-element.14), channel_id=1, source_target_pairs={{0,32},{32,64},{64,96},{1,33},{33,65},{65,97},{2,34},{34,66},{66,9... | collective-permute-start | bytes 1572872 | tf_op jit(solution)/shard_map/ppermute | solution.py:14
  4.5 2.1 %collective-permute-start = (f32[1,64,2048]{2,1,0:T(8,128)S(1)}, f32[1,64,2048]{2,1,0:T(8,128)S(1)}, u32[]{:S(2)}, u32[]{:S(2)}) collective-permute-start(f32[1,64,2048]{2,1,0:T(8,128)S(1)} %get-tuple-element.13), channel_id=1, source_target_pairs={{32,0},{64,32},{96,64},{33,1},{65,33},{97,65},{34,2},{66,34},{98,6... | collective-permute-start | bytes 1572872 | tf_op jit(solution)/shard_map/ppermute | solution.py:15
  6.6 9.4 %collective-permute-done.1 = f32[1,64,2048]{2,1,0:T(8,128)S(1)} collective-permute-done((f32[1,64,2048]{2,1,0:T(8,128)S(1)}, f32[1,64,2048]{2,1,0:T(8,128)S(1)}, u32[]{:S(2)}, u32[]{:S(2)}) %collective-permute-start.1) | collective-permute-done | bytes 524320 | tf_op jit(solution)/shard_map/ppermute | solution.py:14
  16.0 7.4 %constant_dynamic-update-slice_fusion.1 = f32[34,64,2048]{2,1,0:T(8,128)S(1)} fusion(f32[34,64,2048]{2,1,0:T(8,128)S(1)} %constant_dynamic-update-slice_fusion.2, f32[32,64,2048]{2,1,0:T(8,128)} %param.4), kind=kLoop, calls=%fused_computation.37 | loop fusion | bytes 33554432
  23.6 6.1 %copy-done = f32[34,64,2048]{2,1,0:T(8,128)} copy-done((f32[34,64,2048]{2,1,0:T(8,128)}, f32[34,64,2048]{2,1,0:T(8,128)S(1)}, u32[]{:S(2)}) %copy-start) | copy-done | bytes 17825816
  29.7 0.5 fusion.17
  30.2 3.5 %collective-permute-start.2 = (f32[34,1,2048]{2,1,0:T(1,128)S(1)}, f32[34,1,2048]{2,1,0:T(1,128)S(1)}, u32[]{:S(2)}, u32[]{:S(2)}) collective-permute-start(f32[34,1,2048]{2,1,0:T(1,128)S(1)} %get-tuple-element.9), channel_id=1, source_target_pairs={{1,0},{2,1},{3,2},{4,3},{5,4},{6,5},{7,6},{8,7},{9,8},{10,9},{11,1... | collective-permute-start | bytes 835592 | tf_op jit(solution)/shard_map/ppermute | solution.py:15
  33.6 4.2 %collective-permute-start.3 = (f32[34,1,2048]{2,1,0:T(1,128)S(1)}, f32[34,1,2048]{2,1,0:T(1,128)S(1)}, u32[]{:S(2)}, u32[]{:S(2)}) collective-permute-start(f32[34,1,2048]{2,1,0:T(1,128)S(1)} %get-tuple-element.10), channel_id=1, source_target_pairs={{0,1},{1,2},{2,3},{3,4},{4,5},{5,6},{6,7},{7,8},{8,9},{9,10},{10,1... | collective-permute-start | bytes 835592 | tf_op jit(solution)/shard_map/ppermute | solution.py:14
  37.9 0.7 fusion.20
  40.4 0.6 fusion.21
  41.3 68.0 %rsqrt_multiply_fusion = (f32[32,64,2048]{2,1,0:T(8,128)}, f32[32,64,2048]{2,1,0:T(8,128)}, f32[32,64,2048]{2,1,0:T(8,128)}) fusion(f32[32,64,2048]{2,1,0:T(8,128)} %param.4, f32[34,64,2048]{2,1,0:T(8,128)} %copy-done, f32[34,1,2048]{2,1,0:T(1,128)S(1)} %collective-permute-done.3, f32[34,1,2048]{2,1,0:T(1,128)S(1)} %collective-permute-done.2, ...), kind=kOutput, calls=%fused_computation.13 | output fusion | flops 272629760 | bytes 103321088 | tf_op jit(solution)/shard_map/jit(cumsum)/reduce_window_sum | solution.py:41
  109.3 1.1 fusion.9
  110.5 20.6 %multiply_reduce_fusion = f32[3,64,2048]{2,1,0:T(8,128)} fusion(f32[32,64,2048]{2,1,0:T(8,128)} %get-tuple-element.12, f32[3]{0:T(128)S(1)} %get-tuple-element.6, f32[3]{0:T(128)S(1)} %get-tuple-element.7, f32[3]{0:T(128)S(1)} %get-tuple-element.8, f32[32,64,2048]{2,1,0:T(8,128)} %param.4, f32[3]{0:T(128)S(1)} %get-tuple-element.5, ...), kind=kLoop, calls=%fused_computation | loop fusion | flops 112852992 | bytes 51904560 | tf_op jit(solution)/shard_map/reduce_sum | solution.py:44
  131.0 1.6 maximum_bitcast_fusion
  132.6 3.2 %copy.13 = f32[1,4,64,2048]{2,1,0,3:T(4,128)} copy(f32[1,4,64,2048]{3,2,1,0:T(8,128)S(1)} %maximum_bitcast_fusion) | data formatting | bytes 4194304 | tf_op jit(solution)/shard_map/broadcast_in_dim | solution.py:47
  135.8 5.5 %reshape.35 = f32[4,1,131072]{2,1,0:T(1,128)S(1)} reshape(f32[2048,1,4,64]{3,2,1,0:T(4,128)} %bitcast.39) | data formatting | bytes 4194304
  141.2 29.1 %all_to_all.15 = f32[4,1,131072]{2,1,0:T(1,128)} all-to-all(f32[4,1,131072]{2,1,0:T(1,128)S(1)} %reshape.35), channel_id=1, replica_groups=mesh['depth'=4,'tile'=32] {'depth'}, dimensions={0} | all-to-all | bytes 4194304 | tf_op jit(solution)/shard_map/all_to_all | solution.py:47
  170.3 0.5 broadcast.41
  170.8 7.7 %reduce.8 = f32[4,131072]{1,0:T(4,128)S(1)} reduce(f32[4,1,131072]{2,1,0:T(1,128)} %all_to_all.15, f32[]{:T(128)} %broadcast.41), dimensions={1}, to_apply=%all_to_all.11.reduce_sub_computation | reduce | bytes 4194308 | tf_op jit(solution)/shard_map/all_to_all | solution.py:47
  178.5 4.8 %reshape.36 = f32[2048,1,4,64]{3,2,1,0:T(4,128)} reshape(f32[4,131072]{1,0:T(4,128)S(1)} %reduce.8) | data formatting | bytes 4194304
  183.3 3.7 %copy.18 = f32[1,4,64,4,512]{4,3,2,1,0:T(4,128)S(1)} copy(f32[1,4,64,4,512]{2,1,4,3,0:T(4,128)} %bitcast.40) | data formatting | bytes 4194304 | tf_op jit(solution)/shard_map/all_to_all | solution.py:47
  187.0 1.8 fusion.19
  189.2 0.9 fusion.14
  (19 shorter events, 0.7 us)
Async XLA Ops:
  1.3 14.7 %collective-permute-start.1 = (f32[1,64,2048]{2,1,0:T(8,128)S(1)}, f32[1,64,2048]{2,1,0:T(8,128)S(1)}, u32[]{:S(2)}, u32[]{:S(2)}) collective-permute-start(f32[1,64,2048]{2,1,0:T(8,128)S(1)} %get-tuple-element.14), channel_id=1, source_target_pairs={{0,32},{32,64},{64,96},{1,33},{33,65},{65,97},{2,34},{34,66},{66,9... | collective-permute-start | bytes 1572872 | tf_op jit(solution)/shard_map/ppermute | solution.py:14
  4.5 19.0 %collective-permute-start = (f32[1,64,2048]{2,1,0:T(8,128)S(1)}, f32[1,64,2048]{2,1,0:T(8,128)S(1)}, u32[]{:S(2)}, u32[]{:S(2)}) collective-permute-start(f32[1,64,2048]{2,1,0:T(8,128)S(1)} %get-tuple-element.13), channel_id=1, source_target_pairs={{32,0},{64,32},{96,64},{33,1},{65,33},{97,65},{34,2},{66,34},{98,6... | collective-permute-start | bytes 1572872 | tf_op jit(solution)/shard_map/ppermute | solution.py:15
  16.0 21.9 %copy-start.2 = (f32[3]{0:T(128)S(1)}, f32[3]{0:T(128)}, u32[]{:S(2)}) copy-start(f32[3]{0:T(128)} %param.7) | copy-start | bytes 40
  16.0 24.4 %copy-start.3 = (f32[2]{0:T(128)S(1)}, f32[2]{0:T(128)}, u32[]{:S(2)}) copy-start(f32[2]{0:T(128)} %param.5) | copy-start | bytes 28
  16.0 25.0 %copy-start.1 = (f32[3,4]{1,0:T(4,128)S(1)}, f32[3,4]{1,0:T(4,128)}, u32[]{:S(2)}) copy-start(f32[3,4]{1,0:T(4,128)} %param.6) | copy-start | bytes 148
  23.5 6.1 %copy-start = (f32[34,64,2048]{2,1,0:T(8,128)}, f32[34,64,2048]{2,1,0:T(8,128)S(1)}, u32[]{:S(2)}) copy-start(f32[34,64,2048]{2,1,0:T(8,128)S(1)} %constant_dynamic-update-slice_fusion) | copy-start | bytes 53477380
  30.2 11.1 %collective-permute-start.2 = (f32[34,1,2048]{2,1,0:T(1,128)S(1)}, f32[34,1,2048]{2,1,0:T(1,128)S(1)}, u32[]{:S(2)}, u32[]{:S(2)}) collective-permute-start(f32[34,1,2048]{2,1,0:T(1,128)S(1)} %get-tuple-element.9), channel_id=1, source_target_pairs={{1,0},{2,1},{3,2},{4,3},{5,4},{6,5},{7,6},{8,7},{9,8},{10,9},{11,1... | collective-permute-start | bytes 835592 | tf_op jit(solution)/shard_map/ppermute | solution.py:15
  33.6 7.7 %collective-permute-start.3 = (f32[34,1,2048]{2,1,0:T(1,128)S(1)}, f32[34,1,2048]{2,1,0:T(1,128)S(1)}, u32[]{:S(2)}, u32[]{:S(2)}) collective-permute-start(f32[34,1,2048]{2,1,0:T(1,128)S(1)} %get-tuple-element.10), channel_id=1, source_target_pairs={{0,1},{1,2},{2,3},{3,4},{4,5},{5,6},{6,7},{7,8},{8,9},{9,10},{10,1... | collective-permute-start | bytes 835592 | tf_op jit(solution)/shard_map/ppermute | solution.py:14
where the time goes:
time: 192 us; the launch traced here: 190 us
  other arithmetic  100 us (52%)
  local copies, waits for them, and re-layouts  36.3 us (19%)
  blocking collectives  29.1 us (15%)
  starting transfers between devices  13 us (7%)
  waiting for transfers between devices  9.44 us (5%)
  between operations  2.12 us (1%)
    another operation x1, other arithmetic, on_device(): running = jnp.cumsum(sigma, axis=0)  68 us
    all_to_all x1, blocking collectives, on_device(): lax.all_to_all(partial_image[None], 'depth', split_axis=3, concat_axis=0,...  29.1 us
    unnamed x13, local copies, waits for them, and re-layouts  23.9 us
    reduce_sum x1, other arithmetic, on_device(): color = jnp.sum(emitted * weight[None], axis=1)  20.6 us
    ppermute x2, waiting for transfers between devices, with_halo(): before = lax.ppermute(last, axis, up)  9.43 us
    all_to_all x1, other arithmetic, on_device(): lax.all_to_all(partial_image[None], 'depth', split_axis=3, concat_axis=0,...  7.72 us
    ppermute x2, starting transfers between devices, with_halo(): before = lax.ppermute(last, axis, up)  7.42 us
    ppermute x2, starting transfers between devices, with_halo(): after = lax.ppermute(initial, axis, down)  5.56 us
  transfers between devices with their start and end apart: 4, of which 2 were waited for; matrix products, arithmetic and copies ran while one was open for 5% of the time, Pallas kernels for 0%

commit v1 on v0

v1 whole, which is shorter than its diff:
```python
import functools
import math

import jax
import jax.numpy as jnp
from jax import lax
from jax.experimental import pallas as pl
from jax.experimental.pallas import tpu as pltpu
from jax.sharding import PartitionSpec as P

MESH = pl.DeviceIdType.MESH
LANES = 128
SUB = 8
TOP = 8
GROUP = 4
UNROLL = 2


def march(f_ref, j, dst, absorb_ref, color_ref, light_ref, slices, rows):
    lane = lax.broadcasted_iota(jnp.int32, (SUB, LANES), 1)
    first, last = lane == 0, lane == LANES - 1
    base = -absorb_ref[0] * math.log2(math.e)
    slope = -absorb_ref[1] * math.log2(math.e)
    lz, lx, ly = light_ref[0], light_ref[1], light_ref[2]
    for top in range(0, rows, GROUP * SUB):
        starts = [TOP + top + SUB * r for r in range(GROUP)]

        def step(i, carry):
            state = [list(carry[5 * r : 5 * r + 5]) for r in range(GROUP)]
            z0 = 1 + i * UNROLL
            for r, row in enumerate(starts):
                here = [f_ref[j + 1, z0 + u - 1, pl.ds(row, SUB), :] for u in range(UNROLL + 2)]
                for u in range(UNROLL):
                    z = z0 + u
                    below, f, above = here[u], here[u + 1], here[u + 2]
                    dz = above - below
                    dx = f_ref[j + 1, z, pl.ds(row + 1, SUB), :] - f_ref[j + 1, z, pl.ds(row - 1, SUB), :]
                    left = jnp.where(last, f_ref[j, z, pl.ds(row, SUB), :], f)
                    right = jnp.where(first, f_ref[j + 2, z, pl.ds(row, SUB), :], f)
                    dy = pltpu.roll(right, LANES - 1, 1) - pltpu.roll(left, 1, 1)
                    facing = jnp.abs(lz * dz + lx * dx + ly * dy)
                    shade = facing * lax.rsqrt((dz * dz + 4.0) + (dx * dx + dy * dy))
                    f2 = f * f
                    t, m0, m1, m2, m3 = state[r]
                    behind = t * jnp.exp2(base + slope * f2)
                    w0 = (t - behind) * shade
                    w1 = w0 * f
                    state[r] = [behind, m0 + w0, m1 + w1, m2 + w0 * f2, m3 + w1 * f2]
            return tuple(v for s in state for v in s)

        one = jnp.ones((SUB, LANES), jnp.float32)
        zero = jnp.zeros((SUB, LANES), jnp.float32)
        carry = lax.fori_loop(0, slices // UNROLL, step, (one, zero, zero, zero, zero) * GROUP)
        for r in range(GROUP):
            t, m0, m1, m2, m3 = carry[5 * r : 5 * r + 5]
            at = pl.ds(top + SUB * r, SUB)
            for c in range(3):
                dst[c, at, :] = (color_ref[c, 0] * m0 + color_ref[c, 1] * m1) + (
                    color_ref[c, 2] * m2 + color_ref[c, 3] * m3
                )
            dst[3, at, :] = t


def kernel(
    depths, tiles, slices, rows, blocks,
    field, absorb, color, light, out,
    f_ref, mine, image,
    load_sem, z_send, z_recv, x_send, x_recv, i_send, i_recv,
):
    d, t = lax.axis_index("depth"), lax.axis_index("tile")
    per = blocks // depths
    has_below, has_above = d > 0, d < depths - 1
    has_prev, has_next = t > 0, t < tiles - 1

    def load(j):
        return pltpu.make_async_copy(
            field.at[:, :, pl.ds(pl.multiple_of(j * LANES, LANES), LANES)],
            f_ref.at[j + 1, pl.ds(1, slices), pl.ds(TOP, rows), :],
            load_sem.at[j],
        )

    for j in range(blocks):
        load(j).start()

    barrier = pltpu.get_barrier_semaphore()
    for off in range(1, depths):
        pl.semaphore_signal(barrier, inc=1, device_id=(lax.rem(d + off, depths), t), device_id_type=MESH)
    for off in (1, tiles - 1):
        pl.semaphore_signal(barrier, inc=1, device_id=(d, lax.rem(t + off, tiles)), device_id_type=MESH)

    zeros = jnp.zeros((SUB, LANES), jnp.float32)
    for edge in (0, blocks + 1):

        def clear(z, _):
            for row in range(0, rows, SUB):
                f_ref[edge, z + 1, pl.ds(TOP + row, SUB), :] = zeros
            return 0

        lax.fori_loop(0, slices, clear, 0)
    for present, z in ((has_below, 0), (has_above, slices + 1)):

        @pl.when(jnp.logical_not(present))
        def _():
            def clear(j, _):
                for row in range(0, rows, SUB):
                    f_ref[j + 1, z, pl.ds(TOP + row, SUB), :] = zeros
                return 0

            lax.fori_loop(0, blocks, clear, 0)

    for present, row in ((has_prev, TOP - SUB), (has_next, TOP + rows)):

        @pl.when(jnp.logical_not(present))
        def _():
            def clear(j, _):
                for z in range(slices):
                    f_ref[j + 1, z + 1, pl.ds(row, SUB), :] = zeros
                return 0

            lax.fori_loop(0, blocks, clear, 0)

    pl.semaphore_wait(barrier, depths + 1)

    def order(owner_of, s):
        pick = lax.rem(s, depths - 1)
        off = jnp.where(pick == 0, 2, jnp.where(pick == 1, 1, 3))
        owner = lax.rem(owner_of + off, depths)
        own = s >= (depths - 1) * per
        k = jnp.where(own, s - (depths - 1) * per, s // (depths - 1))
        owner = jnp.where(own, owner_of, owner)
        return owner, k, owner * per + k

    def z_copy(way, j):
        src, dst = ((slices - 1, 0), (0, slices + 1))[way]
        return pltpu.make_async_remote_copy(
            src_ref=field.at[src, :, pl.ds(pl.multiple_of(j * LANES, LANES), LANES)],
            dst_ref=f_ref.at[j + 1, dst, pl.ds(TOP, rows), :],
            send_sem=z_send.at[way, j],
            recv_sem=z_recv.at[way, j],
            device_id=(lax.rem(d + (1, depths - 1)[way], depths), t),
            device_id_type=MESH,
        )

    def x_copy(way, j):
        src, dst = ((rows - 1, TOP - 1), (0, TOP + rows))[way]
        return pltpu.make_async_remote_copy(
            src_ref=field.at[:, pl.ds(src, 1), pl.ds(pl.multiple_of(j * LANES, LANES), LANES)],
            dst_ref=f_ref.at[j + 1, pl.ds(1, slices), pl.ds(dst, 1), :],
            send_sem=x_send.at[way, j],
            recv_sem=x_recv.at[way, j],
            device_id=(d, lax.rem(t + (1, tiles - 1)[way], tiles)),
            device_id_type=MESH,
        )

    sends = ((z_copy, 0, has_above, d + 1), (z_copy, 1, has_below, d - 1 + depths),
             (x_copy, 0, has_next, d), (x_copy, 1, has_prev, d))
    recvs = ((z_copy, 0, has_below), (z_copy, 1, has_above), (x_copy, 0, has_prev), (x_copy, 1, has_next))

    def start(s, _):
        for copy, way, present, to in sends:

            @pl.when(present)
            def _():
                copy(way, order(lax.rem(to, depths), s)[2]).start()

        return 0

    lax.fori_loop(0, blocks, start, 0)
    for j in range(blocks):
        load(j).wait()

    def image_copy(s, owner, k):
        return pltpu.make_async_remote_copy(
            src_ref=mine.at[s],
            dst_ref=image.at[d, k],
            send_sem=i_send.at[s],
            recv_sem=i_recv.at[d, k],
            device_id=(owner, t),
            device_id_type=MESH,
        )

    def arrive(j):
        for copy, way, present in recvs:

            @pl.when(present)
            def _():
                copy(way, j).wait_recv()

    def remote(s, _):
        owner, k, j = order(d, s)
        arrive(j)
        march(f_ref, j, mine.at[s], absorb, color, light, slices, rows)
        image_copy(s, owner, k).start()
        return 0

    lax.fori_loop(0, (depths - 1) * per, remote, 0)

    def local(k, _):
        j = d * per + k
        arrive(j)
        march(f_ref, j, image.at[d, k], absorb, color, light, slices, rows)
        return 0

    lax.fori_loop(0, per, local, 0)

    for k in range(per):
        for off in range(1, depths):
            q = lax.rem(d + off, depths)
            pltpu.make_async_remote_copy(
                src_ref=mine.at[0],
                dst_ref=image.at[q, k],
                send_sem=i_send.at[0],
                recv_sem=i_recv.at[q, k],
                device_id=(q, t),
                device_id_type=MESH,
            ).wait_recv()

        def compose(i, _):
            at = pl.ds(pl.multiple_of(i * SUB, SUB), SUB)
            seen = image[0, k, 3, at, :]
            total = [image[0, k, c, at, :] for c in range(3)]
            for q in range(1, depths):
                total = [total[c] + seen * image[q, k, c, at, :] for c in range(3)]
                seen = seen * image[q, k, 3, at, :]
            for c in range(3):
                out[c, at, k * LANES : (k + 1) * LANES] = total[c]
            out[3, at, k * LANES : (k + 1) * LANES] = 1.0 - seen
            return 0

        lax.fori_loop(0, rows // SUB, compose, 0)

    def drain(s, _):
        for copy, way, present, _to in sends:

            @pl.when(present)
            def _():
                copy(way, s).wait_send()

        return 0

    lax.fori_loop(0, blocks, drain, 0)

    def drain_images(s, _):
        image_copy(s, lax.rem(d + 1, depths), 0).wait_send()
        return 0

    lax.fori_loop(0, (depths - 1) * per, drain_images, 0)


def on_device(depths, tiles, field, absorb, color, light):
    slices, rows, columns = field.shape
    blocks = columns // LANES
    per = blocks // depths
    smem = pl.BlockSpec(memory_space=pltpu.SMEM)
    return pl.pallas_call(
        functools.partial(kernel, depths, tiles, slices, rows, blocks),
        out_shape=jax.ShapeDtypeStruct((4, rows, columns // depths), jnp.float32),
        in_specs=[pl.BlockSpec(memory_space=pl.ANY), smem, smem, smem],
        out_specs=pl.BlockSpec(memory_space=pltpu.VMEM),
        scratch_shapes=[
            pltpu.VMEM((blocks + 2, slices + 2, rows + 2 * TOP, LANES), jnp.float32),
            pltpu.VMEM(((depths - 1) * per, 4, rows, LANES), jnp.float32),
            pltpu.VMEM((depths, per, 4, rows, LANES), jnp.float32),
            pltpu.SemaphoreType.DMA((blocks,)),
            pltpu.SemaphoreType.DMA((2, blocks)),
            pltpu.SemaphoreType.DMA((2, blocks)),
            pltpu.SemaphoreType.DMA((2, blocks)),
            pltpu.SemaphoreType.DMA((2, blocks)),
            pltpu.SemaphoreType.DMA(((depths - 1) * per,)),
            pltpu.SemaphoreType.DMA((depths, per)),
        ],
        compiler_params=pltpu.CompilerParams(
            collective_id=0, has_side_effects=True, vmem_limit_bytes=48 << 20
        ),
    )(field, absorb, color, light)


def solution(mesh):
    depths, tiles = mesh.shape["depth"], mesh.shape["tile"]
    return jax.shard_map(
        functools.partial(on_device, depths, tiles),
        mesh=mesh,
        in_specs=(P("depth", "tile", None), P(), P(), P()),
        out_specs=P(None, "tile", "depth"),
        check_vma=False,
    )
```

time: 192 us -> 69.9 us (0.36)
  the two profiles are of different devices: /device:TPU:15 before, /device:TPU:0 now
where the time goes in v1:
time: 69.9 us; the launch traced here: 69.8 us
  Pallas kernels  67 us (96%)
  local copies, waits for them, and re-layouts  2.79 us (4%)
    pallas_call x1, Pallas kernels, on_device(): pl.pallas_call(functools.partial(kernel, depths, tiles, slices, rows, blo...  67 us
    unnamed x7, local copies, waits for them, and re-layouts  2.79 us

profile of v1, /device:TPU:0, one launch (start us, length us, event | category | flops | bytes accessed | tf_op | source)
XLA Modules:
  0.0 69.8 jit_solution(1336166323598543072)
XLA Ops:
  0.0 0.0 copy-start
  0.0 0.7 copy-done
  0.7 0.0 copy-start.1
  0.7 0.7 copy-done.1
  1.3 0.0 copy-start.2
  1.3 0.7 copy-done.2
  2.0 67.0 %shard_map.46 = f32[4,64,512]{2,1,0:T(8,128)S(1)} custom-call(f32[32,64,2048]{2,1,0:T(8,128)} %field.1, f32[2]{0:T(128)S(1)} %copy-done.1, f32[3,4]{1,0:T(4,128)S(1)} %copy-done, f32[3]{0:T(128)S(1)} %copy-done.2), custom_call_target="tpu_custom_call" | custom-call | tf_op jit(solution)/shard_map/pallas_call | solution.py:255
  69.0 0.8 %copy.6 = f32[4,64,512]{2,1,0:T(8,128)} copy(f32[4,64,512]{2,1,0:T(8,128)S(1)} %shard_map.46) | data formatting | bytes 1048576
Async XLA Ops:
  0.0 0.7 copy-start
  0.7 0.7 copy-start.1
  1.3 0.7 copy-start.2

commit v2 on v1

--- a/solution.py
+++ b/solution.py
@@ -12,8 +12,8 @@
 LANES = 128
 SUB = 8
 TOP = 8
-GROUP = 4
-UNROLL = 2
+GROUP = 2
+UNROLL = 16
 
 
 def march(f_ref, j, dst, absorb_ref, color_ref, light_ref, slices, rows):
@@ -25,19 +25,25 @@
     for top in range(0, rows, GROUP * SUB):
         starts = [TOP + top + SUB * r for r in range(GROUP)]
 
-        def step(i, carry):
-            state = [list(carry[5 * r : 5 * r + 5]) for r in range(GROUP)]
-            z0 = 1 + i * UNROLL
+        def sideways(z0):
+            found = []
+            for row in starts:
+                for u in range(UNROLL):
+                    f = f_ref[j + 1, z0 + u, pl.ds(row, SUB), :]
+                    left = jnp.where(last, f_ref[j, z0 + u, pl.ds(row, SUB), :], f)
+                    right = jnp.where(first, f_ref[j + 2, z0 + u, pl.ds(row, SUB), :], f)
+                    found.append(pltpu.roll(right, LANES - 1, 1) - pltpu.roll(left, 1, 1))
+            return found
+
+        def chunk(z0, state, across):
+            state = [list(state[5 * r : 5 * r + 5]) for r in range(GROUP)]
             for r, row in enumerate(starts):
                 here = [f_ref[j + 1, z0 + u - 1, pl.ds(row, SUB), :] for u in range(UNROLL + 2)]
                 for u in range(UNROLL):
-                    z = z0 + u
                     below, f, above = here[u], here[u + 1], here[u + 2]
                     dz = above - below
-                    dx = f_ref[j + 1, z, pl.ds(row + 1, SUB), :] - f_ref[j + 1, z, pl.ds(row - 1, SUB), :]
-                    left = jnp.where(last, f_ref[j, z, pl.ds(row, SUB), :], f)
-                    right = jnp.where(first, f_ref[j + 2, z, pl.ds(row, SUB), :], f)
-                    dy = pltpu.roll(right, LANES - 1, 1) - pltpu.roll(left, 1, 1)
+                    dx = f_ref[j + 1, z0 + u, pl.ds(row + 1, SUB), :] - f_ref[j + 1, z0 + u, pl.ds(row - 1, SUB), :]
+                    dy = across[r * UNROLL + u]
                     facing = jnp.abs(lz * dz + lx * dx + ly * dy)
                     shade = facing * lax.rsqrt((dz * dz + 4.0) + (dx * dx + dy * dy))
                     f2 = f * f
@@ -46,11 +52,19 @@
                     w0 = (t - behind) * shade
                     w1 = w0 * f
                     state[r] = [behind, m0 + w0, m1 + w1, m2 + w0 * f2, m3 + w1 * f2]
-            return tuple(v for s in state for v in s)
+            return [v for s in state for v in s]
+
+        def step(i, carry):
+            z0 = 1 + i * UNROLL
+            ahead = sideways(z0 + UNROLL)
+            return tuple(chunk(z0, carry[: 5 * GROUP], carry[5 * GROUP :]) + ahead)
 
         one = jnp.ones((SUB, LANES), jnp.float32)
         zero = jnp.zeros((SUB, LANES), jnp.float32)
-        carry = lax.fori_loop(0, slices // UNROLL, step, (one, zero, zero, zero, zero) * GROUP)
+        carry = lax.fori_loop(
+            0, slices // UNROLL - 1, step, (one, zero, zero, zero, zero) * GROUP + tuple(sideways(1))
+        )
+        carry = chunk(1 + slices - UNROLL, carry[: 5 * GROUP], carry[5 * GROUP :])
         for r in range(GROUP):
             t, m0, m1, m2, m3 = carry[5 * r : 5 * r + 5]
             at = pl.ds(top + SUB * r, SUB)
@@ -63,8 +77,8 @@
 
 def kernel(
     depths, tiles, slices, rows, blocks,
-    field, absorb, color, light, out,
-    f_ref, mine, image,
+    field, absorb_in, color_in, light_in, out,
+    f_ref, mine, image, absorb, color, light, param_sem,
     load_sem, z_send, z_recv, x_send, x_recv, i_send, i_recv,
 ):
     d, t = lax.axis_index("depth"), lax.axis_index("tile")
@@ -79,6 +93,12 @@
             load_sem.at[j],
         )
 
+    params = [
+        pltpu.make_async_copy(src, dst, param_sem.at[i])
+        for i, (src, dst) in enumerate(((absorb_in, absorb), (color_in, color), (light_in, light)))
+    ]
+    for copy in params:
+        copy.start()
     for j in range(blocks):
         load(j).start()
 
@@ -166,6 +186,8 @@
         return 0
 
     lax.fori_loop(0, blocks, start, 0)
+    for copy in params:
+        copy.wait()
     for j in range(blocks):
         load(j).wait()
 
@@ -251,16 +273,19 @@
     slices, rows, columns = field.shape
     blocks = columns // LANES
     per = blocks // depths
-    smem = pl.BlockSpec(memory_space=pltpu.SMEM)
     return pl.pallas_call(
         functools.partial(kernel, depths, tiles, slices, rows, blocks),
         out_shape=jax.ShapeDtypeStruct((4, rows, columns // depths), jnp.float32),
-        in_specs=[pl.BlockSpec(memory_space=pl.ANY), smem, smem, smem],
+        in_specs=[pl.BlockSpec(memory_space=pl.ANY)] * 4,
         out_specs=pl.BlockSpec(memory_space=pltpu.VMEM),
         scratch_shapes=[
             pltpu.VMEM((blocks + 2, slices + 2, rows + 2 * TOP, LANES), jnp.float32),
             pltpu.VMEM(((depths - 1) * per, 4, rows, LANES), jnp.float32),
             pltpu.VMEM((depths, per, 4, rows, LANES), jnp.float32),
+            pltpu.SMEM((2,), jnp.float32),
+            pltpu.SMEM((3, 4), jnp.float32),
+            pltpu.SMEM((3,), jnp.float32),
+            pltpu.SemaphoreType.DMA((3,)),
             pltpu.SemaphoreType.DMA((blocks,)),
             pltpu.SemaphoreType.DMA((2, blocks)),
             pltpu.SemaphoreType.DMA((2, blocks)),
@@ -270,7 +295,7 @@
             pltpu.SemaphoreType.DMA((depths, per)),
         ],
         compiler_params=pltpu.CompilerParams(
-            collective_id=0, has_side_effects=True, vmem_limit_bytes=48 << 20
+            collective_id=0, has_side_effects=True, vmem_limit_bytes=60 << 20
         ),
     )(field, absorb, color, light)
 

time: 69.9 us -> 43.4 us (0.62)
  the two profiles are of different devices: /device:TPU:0 before, /device:TPU:15 now
where the time goes in v2:
time: 43.4 us; the launch traced here: 43.2 us
  Pallas kernels  41.3 us (95%)
  local copies, waits for them, and re-layouts  1.87 us (4%)
    pallas_call x1, Pallas kernels, on_device(): pl.pallas_call(functools.partial(kernel, depths, tiles, slices, rows, blo...  41.3 us
    unnamed x1, local copies, waits for them, and re-layouts  1.87 us

profile of v2, /device:TPU:15, one launch (start us, length us, event | category | flops | bytes accessed | tf_op | source)
XLA Modules:
  0.0 43.2 jit_solution(350285563474233197)
XLA Ops:
  0.0 41.3 %shard_map.46 = f32[4,64,512]{2,1,0:T(8,128)} custom-call(f32[32,64,2048]{2,1,0:T(8,128)} %field.1, f32[2]{0:T(128)} %absorb_in.1, f32[3,4]{1,0:T(4,128)} %color_in.1, f32[3]{0:T(128)} %light_in.1), custom_call_target="tpu_custom_call" | custom-call | tf_op jit(solution)/shard_map/pallas_call | solution.py:276
  41.4 1.9 %copy.6 = f32[4,64,512]{2,1,0:T(8,128)} copy(f32[4,64,512]{2,1,0:T(8,128)} %shard_map.46) | data formatting | bytes 1048576

commit v3 on v2

v3 whole, which is shorter than its diff:
```python
import functools
import math

import jax
import jax.numpy as jnp
from jax import lax
from jax.experimental import pallas as pl
from jax.experimental.pallas import tpu as pltpu
from jax.sharding import PartitionSpec as P

MESH = pl.DeviceIdType.MESH
LANES = 128
SUB = 8
TOP = 8
Z0 = 2
GROUP = 2
UNROLL = 16
LAG = 4
SPLIT = 3


class Shading:
    def __init__(self, absorb, color, light):
        self.base = -absorb[0] * math.log2(math.e)
        self.slope = -absorb[1] * math.log2(math.e)
        self.light = light[0], light[1], light[2]
        self.color = color

    def facing_and_norm(self, dz, dx, dy):
        lz, lx, ly = self.light
        facing = jnp.abs(lz * dz + lx * dx + ly * dy)
        return facing * lax.rsqrt((dz * dz + 4.0) + (dx * dx + dy * dy))

    def channel(self, c, m0, m1, m2, m3):
        color = self.color
        return (color[c, 0] * m0 + color[c, 1] * m1) + (color[c, 2] * m2 + color[c, 3] * m3)


def sideways(f_ref, j, z, row):
    lane = lax.broadcasted_iota(jnp.int32, (SUB, LANES), 1)
    f = f_ref[j + 1, z, pl.ds(row, SUB), :]
    left = jnp.where(lane == LANES - 1, f_ref[j, z, pl.ds(row, SUB), :], f)
    right = jnp.where(lane == 0, f_ref[j + 2, z, pl.ds(row, SUB), :], f)
    return pltpu.roll(right, LANES - 1, 1) - pltpu.roll(left, 1, 1)


def rowwise(f_ref, j, z, row):
    return f_ref[j + 1, z, pl.ds(row + 1, SUB), :] - f_ref[j + 1, z, pl.ds(row - 1, SUB), :]


def march(f_ref, j, dst, shading, keep_first, keep_last, slices, rows):
    first = shading.base * keep_first, shading.slope * keep_first
    last = shading.base * keep_last, shading.slope * keep_last

    for top in range(0, rows, GROUP * SUB):
        starts = [TOP + top + SUB * r for r in range(GROUP)]

        def across(s0):
            return [sideways(f_ref, j, Z0 + s0 + u, row) for row in starts for u in range(UNROLL)]

        one = jnp.ones((SUB, LANES), jnp.float32)
        zero = jnp.zeros((SUB, LANES), jnp.float32)
        state = [[one, zero, zero, zero, zero] for _ in range(GROUP)]
        ahead = across(0)
        for s0 in range(0, slices, UNROLL):
            now = ahead
            if s0 + UNROLL < slices:
                ahead = across(s0 + UNROLL)
            for r, row in enumerate(starts):
                here = [f_ref[j + 1, Z0 + s0 + u - 1, pl.ds(row, SUB), :] for u in range(UNROLL + 2)]
                for u in range(UNROLL):
                    below, f, above = here[u], here[u + 1], here[u + 2]
                    dx = rowwise(f_ref, j, Z0 + s0 + u, row)
                    shade = shading.facing_and_norm(above - below, dx, now[r * UNROLL + u])
                    base, slope = shading.base, shading.slope
                    if s0 + u == 0:
                        base, slope = first
                    if s0 + u == slices - 1:
                        base, slope = last
                    f2 = f * f
                    t, m0, m1, m2, m3 = state[r]
                    behind = t * jnp.exp2(base + slope * f2)
                    w0 = (t - behind) * shade
                    w1 = w0 * f
                    state[r] = [behind, m0 + w0, m1 + w1, m2 + w0 * f2, m3 + w1 * f2]
        for r in range(GROUP):
            t, *moments = state[r]
            at = pl.ds(top + SUB * r, SUB)
            for c in range(3):
                dst[c, at, :] = shading.channel(c, *moments)
            dst[3, at, :] = t


def march_one(f_ref, j, z, dst, shading, in_front, rows):
    def tile(i, _):
        top = pl.multiple_of(i * SUB, SUB)
        row = top + TOP
        f = f_ref[j + 1, z, pl.ds(row, SUB), :]
        dz = f_ref[j + 1, z + 1, pl.ds(row, SUB), :] - f_ref[j + 1, z - 1, pl.ds(row, SUB), :]
        shade = shading.facing_and_norm(dz, rowwise(f_ref, j, z, row), sideways(f_ref, j, z, row))
        f2 = f * f
        passed = jnp.exp2(shading.base + shading.slope * f2)
        w0 = (1.0 - passed) * shade
        w1 = w0 * f
        at = pl.ds(top, SUB)
        seen = dst[3, at, :]
        one = jnp.ones_like(seen)
        old = jnp.where(in_front, passed, one)
        new = jnp.where(in_front, one, seen)
        for c in range(3):
            dst[c, at, :] = old * dst[c, at, :] + new * shading.channel(c, w0, w1, w0 * f2, w1 * f2)
        dst[3, at, :] = seen * passed
        return 0

    lax.fori_loop(0, rows // SUB, tile, 0)


def kernel(
    depths, tiles, slices, rows, blocks,
    field, absorb_in, color_in, light_in, out,
    f_ref, image, relay, frame, absorb, color, light,
    param_sem, load_sem, z_send, z_recv, e_send, e_recv, x_send, x_recv, y_send, y_recv,
    i_send, r_recv, i_recv, out_sem,
):
    d, t = lax.axis_index("depth"), lax.axis_index("tile")
    per = blocks // depths
    sent = (depths - 1) * per
    up_d, down_d = lax.rem(d + 1, depths), lax.rem(d + depths - 1, depths)
    next_t, prev_t = lax.rem(t + 1, tiles), lax.rem(t + tiles - 1, tiles)
    has_prev, has_next = t > 0, t < tiles - 1
    outer = jnp.logical_or(d == 0, d == depths - 1)

    params = [
        pltpu.make_async_copy(src, dst, param_sem.at[i])
        for i, (src, dst) in enumerate(((absorb_in, absorb), (color_in, color), (light_in, light)))
    ]

    def columns(j):
        return pl.ds(pl.multiple_of(j * LANES, LANES), LANES)

    def load(j):
        return pltpu.make_async_copy(
            field.at[:, :, columns(j)],
            f_ref.at[j + 1, pl.ds(Z0, slices), pl.ds(TOP, rows), :],
            load_sem.at[j],
        )

    barrier = pltpu.get_barrier_semaphore()
    for peer in ((up_d, t), (down_d, t), (d, next_t), (d, prev_t)):
        pl.semaphore_signal(barrier, inc=1, device_id=peer, device_id_type=MESH)
    for copy in params:
        copy.start()
    for j in range(blocks):
        load(j).start()

    zeros = jnp.zeros((SUB, LANES), jnp.float32)
    for edge in (0, blocks + 1):

        def clear(z, _):
            for row in range(0, rows, SUB):
                f_ref[edge, z, pl.ds(TOP + row, SUB), :] = zeros
            return 0

        lax.fori_loop(0, slices + 2 * Z0, clear, 0)
    for present, z, j0, j1 in (
        (d <= 1, Z0 - 1, 0, per),
        (d == 0, Z0 - 1, per, blocks),
        (d >= depths - 2, Z0 + slices, sent, blocks),
        (d == depths - 1, Z0 + slices, 0, sent),
    ):

        @pl.when(present)
        def _():
            def clear(j, _):
                for row in range(0, rows, SUB):
                    f_ref[j + 1, z, pl.ds(TOP + row, SUB), :] = zeros
                return 0

            lax.fori_loop(j0, j1, clear, 0)

    for present, row in ((has_prev, TOP - SUB), (has_next, TOP + rows)):

        @pl.when(jnp.logical_not(present))
        def _():
            def clear(j, _):
                for z in range(slices + 2 * Z0):
                    f_ref[j + 1, z, pl.ds(row, SUB), :] = zeros
                return 0

            lax.fori_loop(0, blocks, clear, 0)

    pl.semaphore_wait(barrier, 4)

    def order(me, s):
        far, own = s < per, s >= sent
        way = jnp.where(far, 0, jnp.where(own, 3, 1 + lax.rem(s, 2)))
        k = jnp.where(far, s, jnp.where(own, s - sent, (s - per) // 2))
        off = jnp.where(way == 0, 2, jnp.where(way == 1, 1, jnp.where(way == 2, depths - 1, 0)))
        return way, lax.rem(me + off, depths), k

    def block(me, s):
        _, owner, k = order(me, s)
        return owner * per + k

    def shifted(me, j):
        return j // per == jnp.where(me < depths // 2, 0, depths - 1)

    def sends_up(me, j):
        return jnp.logical_and(me < depths - 1, jnp.logical_not(jnp.logical_and(me == 0, shifted(me, j))))

    def sends_down(me, j):
        return jnp.logical_and(me > 0, jnp.logical_not(jnp.logical_and(me == depths - 1, shifted(me, j))))

    def z_copy(way, j):
        src, dst = ((slices - 1, Z0 - 1), (0, Z0 + slices))[way]
        return pltpu.make_async_remote_copy(
            src_ref=field.at[src, :, columns(j)],
            dst_ref=f_ref.at[j + 1, dst, pl.ds(TOP, rows), :],
            send_sem=z_send.at[way, j],
            recv_sem=z_recv.at[way, j],
            device_id=((up_d, down_d)[way], t),
            device_id_type=MESH,
        )

    def e_copy(k):
        up = d == depths - 2
        j = jnp.where(up, sent, 0) + k
        return pltpu.make_async_remote_copy(
            src_ref=field.at[jnp.where(up, slices - 2, 1), :, columns(j)],
            dst_ref=f_ref.at[j + 1, jnp.where(up, Z0 - 2, Z0 + slices + 1), pl.ds(TOP, rows), :],
            send_sem=e_send.at[k],
            recv_sem=e_recv.at[k],
            device_id=(jnp.where(up, up_d, down_d), t),
            device_id_type=MESH,
        )

    def e_wait(k):
        low = d == 0
        j = d * per + k
        pltpu.make_async_remote_copy(
            src_ref=field.at[0, :, columns(j)],
            dst_ref=f_ref.at[j + 1, jnp.where(low, Z0 + slices + 1, Z0 - 2), pl.ds(TOP, rows), :],
            send_sem=e_send.at[k],
            recv_sem=e_recv.at[k],
            device_id=(jnp.where(low, up_d, down_d), t),
            device_id_type=MESH,
        ).wait_recv()

    def x_copy(way, j):
        src, dst = ((rows - 1, TOP - 1), (0, TOP + rows))[way]
        return pltpu.make_async_remote_copy(
            src_ref=field.at[:, pl.ds(src, 1), columns(j)],
            dst_ref=f_ref.at[j + 1, pl.ds(Z0, slices), pl.ds(dst, 1), :],
            send_sem=x_send.at[way, j],
            recv_sem=x_recv.at[way, j],
            device_id=(d, (next_t, prev_t)[way]),
            device_id_type=MESH,
        )

    extra_z = jnp.where(d == 0, Z0 + slices, Z0 - 1)

    def y_copy(way, k):
        src, dst = ((TOP + rows - 1, TOP - 1), (TOP, TOP + rows))[way]
        j = d * per + k
        return pltpu.make_async_remote_copy(
            src_ref=f_ref.at[j + 1, extra_z, pl.ds(src, 1), :],
            dst_ref=f_ref.at[j + 1, extra_z, pl.ds(dst, 1), :],
            send_sem=y_send.at[way, k],
            recv_sem=y_recv.at[way, k],
            device_id=(d, (next_t, prev_t)[way]),
            device_id_type=MESH,
        )

    def start(s, _):
        j = block(up_d, s)

        @pl.when(sends_up(d, j))
        def _():
            z_copy(0, j).start()

        j = block(down_d, s)

        @pl.when(sends_down(d, j))
        def _():
            z_copy(1, j).start()

        j = block(d, s)

        @pl.when(has_next)
        def _():
            x_copy(0, j).start()

        @pl.when(has_prev)
        def _():
            x_copy(1, j).start()

        return 0

    lax.fori_loop(0, blocks, start, 0)

    @pl.when(jnp.logical_not(outer))
    def _():
        for k in range(per):
            e_copy(k).start()

    for copy in params:
        copy.wait()
    for j in range(blocks):
        load(j).wait()
    shading = Shading(absorb, color, light)

    def relays_up(me, k):
        inner = jnp.where(me == 1, k < SPLIT, k >= SPLIT)
        return jnp.logical_or(me == 0, jnp.logical_and(me < depths - 1, inner))

    def merges(way, k):
        from_below = jnp.logical_and(d > 0, relays_up(d - 1, k))
        from_above = jnp.logical_and(d < depths - 1, jnp.logical_not(relays_up(d + 1, k)))
        return jnp.logical_or(
            jnp.logical_and(way == 1, from_below), jnp.logical_and(way == 2, from_above)
        )

    def place(me, way, k):
        inner = jnp.where(way == 1, 0, jnp.where(way == 2, 2, 1))
        low = jnp.where(way == 1, 2, jnp.where(way == 2, 1, 0))
        high = jnp.where(way == 1, 1, jnp.where(way == 2, 0, 2))
        return sent + jnp.where(me == 0, low, jnp.where(me == depths - 1, high, inner)) * per + k

    def relay_copy(up, s, k):
        way = jnp.where(up, 0, 1)
        return pltpu.make_async_remote_copy(
            src_ref=image.at[s],
            dst_ref=relay.at[way, k],
            send_sem=i_send.at[s],
            recv_sem=r_recv.at[way, k],
            device_id=(jnp.where(up, up_d, down_d), t),
            device_id_type=MESH,
        )

    def image_copy(way, s, k):
        up = way == 1
        owner = jnp.where(up, up_d, down_d)
        return pltpu.make_async_remote_copy(
            src_ref=image.at[s],
            dst_ref=image.at[place(owner, way, k)],
            send_sem=i_send.at[s],
            recv_sem=i_recv.at[way - 1, k],
            device_id=(owner, t),
            device_id_type=MESH,
        )

    def merge(way, s, k):
        relay_copy(way == 1, s, k).wait_recv()
        front = way == 1

        def tile(i, _):
            at = pl.ds(pl.multiple_of(i * SUB, SUB), SUB)
            mine, other = image[s, 3, at, :], relay[way - 1, k, 3, at, :]
            one = jnp.ones_like(mine)
            a, b = jnp.where(front, other, one), jnp.where(front, one, mine)
            for c in range(3):
                image[s, c, at, :] = a * image[s, c, at, :] + b * relay[way - 1, k, c, at, :]
            image[s, 3, at, :] = mine * other
            return 0

        lax.fori_loop(0, rows // SUB, tile, 0)

    def step(s, _):
        way, owner, k = order(d, s)
        j = owner * per + k
        own = way == 3
        handed = jnp.logical_and(outer, own)

        @pl.when(jnp.logical_and(d > 0, jnp.logical_and(sends_up(d - 1, j), jnp.logical_not(handed))))
        def _():
            z_copy(0, j).wait_recv()

        @pl.when(jnp.logical_and(d < depths - 1, jnp.logical_and(sends_down(d + 1, j), jnp.logical_not(handed))))
        def _():
            z_copy(1, j).wait_recv()

        @pl.when(has_prev)
        def _():
            x_copy(0, j).wait_recv()

        @pl.when(has_next)
        def _():
            x_copy(1, j).wait_recv()

        @pl.when(jnp.logical_and(outer, s == sent - 2))
        def _():
            for i in range(per):

                @pl.when(d == 0)
                def _():
                    z_copy(1, d * per + i).wait_recv()

                @pl.when(d > 0)
                def _():
                    z_copy(0, d * per + i).wait_recv()

                @pl.when(has_next)
                def _():
                    y_copy(0, i).start()

                @pl.when(has_prev)
                def _():
                    y_copy(1, i).start()

        shift = shifted(d, j)
        keep_first = jnp.where(jnp.logical_and(d == 1, shift), 0.0, 1.0)
        keep_last = jnp.where(jnp.logical_and(d == depths - 2, shift), 0.0, 1.0)
        slot = jnp.where(own, place(d, 3, k), s)
        march(f_ref, j, image.at[slot], shading, keep_first, keep_last, slices, rows)

        @pl.when(way == 0)
        def _():
            relay_copy(relays_up(d, k), s, k).start()

        near = jnp.logical_or(way == 1, way == 2)

        @pl.when(jnp.logical_and(near, jnp.logical_not(merges(way, k))))
        def _():
            image_copy(way, s, k).start()

        late = jnp.maximum(s - LAG, 0)
        late_way, _, late_k = order(d, late)
        due = jnp.logical_and(s - LAG >= per, s - LAG < sent)

        @pl.when(jnp.logical_and(due, merges(late_way, late_k)))
        def _():
            merge(late_way, late, late_k)
            image_copy(late_way, late, late_k).start()

        @pl.when(handed)
        def _():
            e_wait(k)

            @pl.when(has_prev)
            def _():
                y_copy(0, k).wait_recv()

            @pl.when(has_next)
            def _():
                y_copy(1, k).wait_recv()

            march_one(f_ref, j, extra_z, image.at[slot], shading, d > 0, rows)

        return 0

    lax.fori_loop(0, blocks, step, 0)

    def finished(k):
        return pltpu.make_async_copy(frame.at[k], out.at[:, :, columns(k)], out_sem.at[k])

    for k in range(per):
        for way in (1, 2):
            pltpu.make_async_remote_copy(
                src_ref=image.at[0],
                dst_ref=image.at[place(d, way, k)],
                send_sem=i_send.at[0],
                recv_sem=i_recv.at[way - 1, k],
                device_id=(up_d, t),
                device_id_type=MESH,
            ).wait_recv()

        def compose(i, _):
            at = pl.ds(pl.multiple_of(i * SUB, SUB), SUB)
            seen = image[sent + k, 3, at, :]
            total = [image[sent + k, c, at, :] for c in range(3)]
            for q in (sent + per + k, sent + 2 * per + k):
                total = [total[c] + seen * image[q, c, at, :] for c in range(3)]
                seen = seen * image[q, 3, at, :]
            for c in range(3):
                frame[k, c, at, :] = total[c]
            frame[k, 3, at, :] = 1.0 - seen
            return 0

        lax.fori_loop(0, rows // SUB, compose, 0)
        finished(k).start()

    def drain(j, _):
        @pl.when(sends_up(d, j))
        def _():
            z_copy(0, j).wait_send()

        @pl.when(sends_down(d, j))
        def _():
            z_copy(1, j).wait_send()

        @pl.when(has_next)
        def _():
            x_copy(0, j).wait_send()

        @pl.when(has_prev)
        def _():
            x_copy(1, j).wait_send()

        return 0

    lax.fori_loop(0, blocks, drain, 0)

    def drain_images(s, _):
        relay_copy(d == 0, s, 0).wait_send()
        return 0

    lax.fori_loop(0, sent, drain_images, 0)

    for k in range(per):

        @pl.when(jnp.logical_not(outer))
        def _():
            e_copy(k).wait_send()

        @pl.when(jnp.logical_and(outer, has_next))
        def _():
            y_copy(0, k).wait_send()

        @pl.when(jnp.logical_and(outer, has_prev))
        def _():
            y_copy(1, k).wait_send()

    for k in range(per):
        finished(k).wait()


def on_device(depths, tiles, field, absorb, color, light):
    slices, rows, columns = field.shape
    blocks = columns // LANES
    per = blocks // depths
    sent = (depths - 1) * per
    dma = pltpu.SemaphoreType.DMA
    return pl.pallas_call(
        functools.partial(kernel, depths, tiles, slices, rows, blocks),
        out_shape=jax.ShapeDtypeStruct((4, rows, columns // depths), jnp.float32),
        in_specs=[pl.BlockSpec(memory_space=pl.ANY)] * 4,
        out_specs=pl.BlockSpec(memory_space=pl.ANY),
        scratch_shapes=[
            pltpu.VMEM((blocks + 2, slices + 2 * Z0, rows + 2 * TOP, LANES), jnp.float32),
            pltpu.VMEM((sent + 3 * per, 4, rows, LANES), jnp.float32),
            pltpu.VMEM((2, per, 4, rows, LANES), jnp.float32),
            pltpu.VMEM((per, 4, rows, LANES), jnp.float32),
            pltpu.SMEM((2,), jnp.float32),
            pltpu.SMEM((3, 4), jnp.float32),
            pltpu.SMEM((3,), jnp.float32),
            dma((3,)),
            dma((blocks,)),
            dma((2, blocks)),
            dma((2, blocks)),
            dma((per,)),
            dma((per,)),
            dma((2, blocks)),
            dma((2, blocks)),
            dma((2, per)),
            dma((2, per)),
            dma((sent,)),
            dma((2, per)),
            dma((2, per)),
            dma((per,)),
        ],
        compiler_params=pltpu.CompilerParams(
            collective_id=0, has_side_effects=True, vmem_limit_bytes=60 << 20
        ),
    )(field, absorb, color, light)


def solution(mesh):
    depths, tiles = mesh.shape["depth"], mesh.shape["tile"]
    return jax.shard_map(
        functools.partial(on_device, depths, tiles),
        mesh=mesh,
        in_specs=(P("depth", "tile", None), P(), P(), P()),
        out_specs=P(None, "tile", "depth"),
        check_vma=False,
    )
```

time: 43.4 us -> 40.3 us (0.929)
  Pallas kernels: 41.3 us -> 38.3 us
    pallas_call x1, Pallas kernels: 41.3 us -> 38.3 us  [on_device(): pl.pallas_call(functools.partial(kernel, depths, tiles, slices, rows, blo...]
where the time goes in v3:
time: 40.3 us; the launch traced here: 40.2 us
  Pallas kernels  38.3 us (95%)
  local copies, waits for them, and re-layouts  1.87 us (5%)
    pallas_call x1, Pallas kernels, on_device(): pl.pallas_call(functools.partial(kernel, depths, tiles, slices, rows, blo...  38.3 us
    unnamed x1, local copies, waits for them, and re-layouts  1.87 us

profile of v3, /device:TPU:15, one launch (start us, length us, event | category | flops | bytes accessed | tf_op | source)
XLA Modules:
  0.0 40.2 jit_solution(6784828095499010783)
XLA Ops:
  0.0 38.3 %shard_map.46 = f32[4,64,512]{2,1,0:T(8,128)} custom-call(f32[32,64,2048]{2,1,0:T(8,128)} %field.1, f32[2]{0:T(128)} %absorb_in.1, f32[3,4]{1,0:T(4,128)} %color_in.1, f32[3]{0:T(128)} %light_in.1), custom_call_target="tpu_custom_call" | custom-call | tf_op jit(solution)/shard_map/pallas_call | solution.py:533
  38.3 1.9 %copy.6 = f32[4,64,512]{2,1,0:T(8,128)} copy(f32[4,64,512]{2,1,0:T(8,128)} %shard_map.46) | data formatting | bytes 1048576

commit v4 on v3

--- a/solution.py
+++ b/solution.py
@@ -118,9 +118,9 @@
 def kernel(
     depths, tiles, slices, rows, blocks,
     field, absorb_in, color_in, light_in, out,
-    f_ref, image, relay, frame, absorb, color, light,
+    f_ref, image, relay, absorb, color, light,
     param_sem, load_sem, z_send, z_recv, e_send, e_recv, x_send, x_recv, y_send, y_recv,
-    i_send, r_recv, i_recv, out_sem,
+    i_send, r_recv, i_recv,
 ):
     d, t = lax.axis_index("depth"), lax.axis_index("tile")
     per = blocks // depths
@@ -146,8 +146,14 @@
         )
 
     barrier = pltpu.get_barrier_semaphore()
-    for peer in ((up_d, t), (down_d, t), (d, next_t), (d, prev_t)):
-        pl.semaphore_signal(barrier, inc=1, device_id=peer, device_id_type=MESH)
+    for peer in (up_d, down_d):
+        pl.semaphore_signal(barrier, inc=1, device_id=(peer, t), device_id_type=MESH)
+    for present, peer in ((has_next, next_t), (has_prev, prev_t)):
+
+        @pl.when(present)
+        def _():
+            pl.semaphore_signal(barrier, inc=1, device_id=(d, peer), device_id_type=MESH)
+
     for copy in params:
         copy.start()
     for j in range(blocks):
@@ -189,7 +195,8 @@
 
             lax.fori_loop(0, blocks, clear, 0)
 
-    pl.semaphore_wait(barrier, 4)
+    beside = has_prev.astype(jnp.int32) + has_next.astype(jnp.int32)
+    pl.semaphore_wait(barrier, 2 + beside)
 
     def order(me, s):
         far, own = s < per, s >= sent
@@ -449,9 +456,6 @@
         return 0
 
     lax.fori_loop(0, blocks, step, 0)
-
-    def finished(k):
-        return pltpu.make_async_copy(frame.at[k], out.at[:, :, columns(k)], out_sem.at[k])
 
     for k in range(per):
         for way in (1, 2):
@@ -472,12 +476,11 @@
                 total = [total[c] + seen * image[q, c, at, :] for c in range(3)]
                 seen = seen * image[q, 3, at, :]
             for c in range(3):
-                frame[k, c, at, :] = total[c]
-            frame[k, 3, at, :] = 1.0 - seen
+                out[c, at, k * LANES : (k + 1) * LANES] = total[c]
+            out[3, at, k * LANES : (k + 1) * LANES] = 1.0 - seen
             return 0
 
         lax.fori_loop(0, rows // SUB, compose, 0)
-        finished(k).start()
 
     def drain(j, _):
         @pl.when(sends_up(d, j))
@@ -519,9 +522,6 @@
         @pl.when(jnp.logical_and(outer, has_prev))
         def _():
             y_copy(1, k).wait_send()
-
-    for k in range(per):
-        finished(k).wait()
 
 
 def on_device(depths, tiles, field, absorb, color, light):
@@ -532,14 +532,13 @@
     dma = pltpu.SemaphoreType.DMA
     return pl.pallas_call(
         functools.partial(kernel, depths, tiles, slices, rows, blocks),
-        out_shape=jax.ShapeDtypeStruct((4, rows, columns // depths), jnp.float32),
+        out_shape=pltpu.VMEM((4, rows, columns // depths), jnp.float32),
         in_specs=[pl.BlockSpec(memory_space=pl.ANY)] * 4,
-        out_specs=pl.BlockSpec(memory_space=pl.ANY),
+        out_specs=pl.BlockSpec(memory_space=pltpu.VMEM),
         scratch_shapes=[
             pltpu.VMEM((blocks + 2, slices + 2 * Z0, rows + 2 * TOP, LANES), jnp.float32),
             pltpu.VMEM((sent + 3 * per, 4, rows, LANES), jnp.float32),
             pltpu.VMEM((2, per, 4, rows, LANES), jnp.float32),
-            pltpu.VMEM((per, 4, rows, LANES), jnp.float32),
             pltpu.SMEM((2,), jnp.float32),
             pltpu.SMEM((3, 4), jnp.float32),
             pltpu.SMEM((3,), jnp.float32),
@@ -556,10 +555,9 @@
             dma((sent,)),
             dma((2, per)),
             dma((2, per)),
-            dma((per,)),
         ],
         compiler_params=pltpu.CompilerParams(
-            collective_id=0, has_side_effects=True, vmem_limit_bytes=60 << 20
+            collective_id=0, has_side_effects=True, vmem_limit_bytes=55 << 20
         ),
     )(field, absorb, color, light)
 

time: 40.3 us -> 38.9 us (0.965)
  local copies, waits for them, and re-layouts: 1.87 us -> 0.8 us
    unnamed x1, local copies, waits for them, and re-layouts: 1.87 us -> 0.8 us
where the time goes in v4:
time: 38.9 us; the launch traced here: 38.8 us
  Pallas kernels  38 us (98%)
  local copies, waits for them, and re-layouts  0.8 us (2%)
    pallas_call x1, Pallas kernels, on_device(): pl.pallas_call(functools.partial(kernel, depths, tiles, slices, rows, blo...  38 us
    unnamed x1, local copies, waits for them, and re-layouts  0.8 us

profile of v4, /device:TPU:15, one launch (start us, length us, event | category | flops | bytes accessed | tf_op | source)
XLA Modules:
  0.0 38.8 jit_solution(9718105546016247299)
XLA Ops:
  0.0 38.0 %shard_map.46 = f32[4,64,512]{2,1,0:T(8,128)S(1)} custom-call(f32[32,64,2048]{2,1,0:T(8,128)} %field.1, f32[2]{0:T(128)} %absorb_in.1, f32[3,4]{1,0:T(4,128)} %color_in.1, f32[3]{0:T(128)} %light_in.1), custom_call_target="tpu_custom_call" | custom-call | tf_op jit(solution)/shard_map/pallas_call | solution.py:533
  38.0 0.8 %copy.6 = f32[4,64,512]{2,1,0:T(8,128)} copy(f32[4,64,512]{2,1,0:T(8,128)S(1)} %shard_map.46) | data formatting | bytes 1048576

commit v5 on v4

--- a/solution.py
+++ b/solution.py
@@ -16,7 +16,8 @@
 GROUP = 2
 UNROLL = 16
 LAG = 4
-SPLIT = 3
+SPLIT = 2
+CUT = 48
 
 
 class Shading:
@@ -92,8 +93,7 @@
 
 
 def march_one(f_ref, j, z, dst, shading, in_front, rows):
-    def tile(i, _):
-        top = pl.multiple_of(i * SUB, SUB)
+    def tile(top):
         row = top + TOP
         f = f_ref[j + 1, z, pl.ds(row, SUB), :]
         dz = f_ref[j + 1, z + 1, pl.ds(row, SUB), :] - f_ref[j + 1, z - 1, pl.ds(row, SUB), :]
@@ -110,9 +110,9 @@
         for c in range(3):
             dst[c, at, :] = old * dst[c, at, :] + new * shading.channel(c, w0, w1, w0 * f2, w1 * f2)
         dst[3, at, :] = seen * passed
-        return 0
-
-    lax.fori_loop(0, rows // SUB, tile, 0)
+
+    for top in range(0, rows, SUB):
+        tile(top)
 
 
 def kernel(
@@ -169,10 +169,11 @@
 
         lax.fori_loop(0, slices + 2 * Z0, clear, 0)
     for present, z, j0, j1 in (
-        (d <= 1, Z0 - 1, 0, per),
-        (d == 0, Z0 - 1, per, blocks),
-        (d >= depths - 2, Z0 + slices, sent, blocks),
-        (d == depths - 1, Z0 + slices, 0, sent),
+        (d == 0, Z0 - 1, 0, blocks),
+        (d == 1, Z0 - 1, 0, per),
+        (d == 1, Z0 - 1, 2 * per - 1, 2 * per),
+        (d == depths - 2, Z0 + slices, sent - 1, blocks),
+        (d == depths - 1, Z0 + slices, 0, blocks),
     ):
 
         @pl.when(present)
@@ -210,7 +211,11 @@
         return owner * per + k
 
     def shifted(me, j):
-        return j // per == jnp.where(me < depths // 2, 0, depths - 1)
+        low = jnp.logical_or(j < per, j == 2 * per - 1)
+        return jnp.where(me < depths // 2, low, j >= sent - 1)
+
+    def taken(high, i):
+        return jnp.where(high, sent - 1 + i, jnp.where(i < per, i, 2 * per - 1))
 
     def sends_up(me, j):
         return jnp.logical_and(me < depths - 1, jnp.logical_not(jnp.logical_and(me == 0, shifted(me, j))))
@@ -231,7 +236,7 @@
 
     def e_copy(k):
         up = d == depths - 2
-        j = jnp.where(up, sent, 0) + k
+        j = taken(up, k)
         return pltpu.make_async_remote_copy(
             src_ref=field.at[jnp.where(up, slices - 2, 1), :, columns(j)],
             dst_ref=f_ref.at[j + 1, jnp.where(up, Z0 - 2, Z0 + slices + 1), pl.ds(TOP, rows), :],
@@ -243,7 +248,7 @@
 
     def e_wait(k):
         low = d == 0
-        j = d * per + k
+        j = taken(d > 0, k)
         pltpu.make_async_remote_copy(
             src_ref=field.at[0, :, columns(j)],
             dst_ref=f_ref.at[j + 1, jnp.where(low, Z0 + slices + 1, Z0 - 2), pl.ds(TOP, rows), :],
@@ -268,7 +273,7 @@
 
     def y_copy(way, k):
         src, dst = ((TOP + rows - 1, TOP - 1), (TOP, TOP + rows))[way]
-        j = d * per + k
+        j = taken(d > 0, k)
         return pltpu.make_async_remote_copy(
             src_ref=f_ref.at[j + 1, extra_z, pl.ds(src, 1), :],
             dst_ref=f_ref.at[j + 1, extra_z, pl.ds(dst, 1), :],
@@ -307,7 +312,7 @@
 
     @pl.when(jnp.logical_not(outer))
     def _():
-        for k in range(per):
+        for k in range(per + 1):
             e_copy(k).start()
 
     for copy in params:
@@ -316,16 +321,20 @@
         load(j).wait()
     shading = Shading(absorb, color, light)
 
-    def relays_up(me, k):
-        inner = jnp.where(me == 1, k < SPLIT, k >= SPLIT)
+    def relays_up(me, k, part):
+        through = jnp.logical_or(k < SPLIT, jnp.logical_and(k == SPLIT, part == 0))
+        inner = jnp.where(me == 1, through, jnp.logical_not(through))
         return jnp.logical_or(me == 0, jnp.logical_and(me < depths - 1, inner))
 
-    def merges(way, k):
-        from_below = jnp.logical_and(d > 0, relays_up(d - 1, k))
-        from_above = jnp.logical_and(d < depths - 1, jnp.logical_not(relays_up(d + 1, k)))
+    def merges(way, k, part):
+        from_below = jnp.logical_and(d > 0, relays_up(d - 1, k, part))
+        from_above = jnp.logical_and(d < depths - 1, jnp.logical_not(relays_up(d + 1, k, part)))
         return jnp.logical_or(
             jnp.logical_and(way == 1, from_below), jnp.logical_and(way == 2, from_above)
         )
+
+    def merges_any(way, k):
+        return jnp.logical_or(merges(way, k, 0), merges(way, k, 1))
 
     def place(me, way, k):
         inner = jnp.where(way == 1, 0, jnp.where(way == 2, 2, 1))
@@ -333,13 +342,16 @@
         high = jnp.where(way == 1, 1, jnp.where(way == 2, 0, 2))
         return sent + jnp.where(me == 0, low, jnp.where(me == depths - 1, high, inner)) * per + k
 
-    def relay_copy(up, s, k):
+    parts = ((0, CUT), (CUT, rows - CUT))
+
+    def relay_copy(up, s, k, part):
         way = jnp.where(up, 0, 1)
+        at = pl.ds(*parts[part])
         return pltpu.make_async_remote_copy(
-            src_ref=image.at[s],
-            dst_ref=relay.at[way, k],
-            send_sem=i_send.at[s],
-            recv_sem=r_recv.at[way, k],
+            src_ref=image.at[s, :, at, :],
+            dst_ref=relay.at[way, k, :, at, :],
+            send_sem=i_send.at[part, s],
+            recv_sem=r_recv.at[way, k, part],
             device_id=(jnp.where(up, up_d, down_d), t),
             device_id_type=MESH,
         )
@@ -350,39 +362,38 @@
         return pltpu.make_async_remote_copy(
             src_ref=image.at[s],
             dst_ref=image.at[place(owner, way, k)],
-            send_sem=i_send.at[s],
+            send_sem=i_send.at[0, s],
             recv_sem=i_recv.at[way - 1, k],
             device_id=(owner, t),
             device_id_type=MESH,
         )
 
-    def merge(way, s, k):
-        relay_copy(way == 1, s, k).wait_recv()
+    def merge(way, s, k, part):
+        relay_copy(way == 1, s, k, part).wait_recv()
         front = way == 1
-
-        def tile(i, _):
-            at = pl.ds(pl.multiple_of(i * SUB, SUB), SUB)
+        top, count = parts[part]
+        for row in range(top, top + count, SUB):
+            at = pl.ds(row, SUB)
             mine, other = image[s, 3, at, :], relay[way - 1, k, 3, at, :]
             one = jnp.ones_like(mine)
             a, b = jnp.where(front, other, one), jnp.where(front, one, mine)
             for c in range(3):
                 image[s, c, at, :] = a * image[s, c, at, :] + b * relay[way - 1, k, c, at, :]
             image[s, 3, at, :] = mine * other
-            return 0
-
-        lax.fori_loop(0, rows // SUB, tile, 0)
 
     def step(s, _):
         way, owner, k = order(d, s)
         j = owner * per + k
         own = way == 3
-        handed = jnp.logical_and(outer, own)
-
-        @pl.when(jnp.logical_and(d > 0, jnp.logical_and(sends_up(d - 1, j), jnp.logical_not(handed))))
+        shift = shifted(d, j)
+        handed = jnp.logical_and(outer, shift)
+        waited = jnp.logical_and(outer, own)
+
+        @pl.when(jnp.logical_and(d > 0, jnp.logical_and(sends_up(d - 1, j), jnp.logical_not(waited))))
         def _():
             z_copy(0, j).wait_recv()
 
-        @pl.when(jnp.logical_and(d < depths - 1, jnp.logical_and(sends_down(d + 1, j), jnp.logical_not(handed))))
+        @pl.when(jnp.logical_and(d < depths - 1, jnp.logical_and(sends_down(d + 1, j), jnp.logical_not(waited))))
         def _():
             z_copy(1, j).wait_recv()
 
@@ -394,7 +405,7 @@
         def _():
             x_copy(1, j).wait_recv()
 
-        @pl.when(jnp.logical_and(outer, s == sent - 2))
+        @pl.when(jnp.logical_and(outer, s == sent))
         def _():
             for i in range(per):
 
@@ -406,6 +417,8 @@
                 def _():
                     z_copy(0, d * per + i).wait_recv()
 
+            for i in range(per + 1):
+
                 @pl.when(has_next)
                 def _():
                     y_copy(0, i).start()
@@ -414,7 +427,6 @@
                 def _():
                     y_copy(1, i).start()
 
-        shift = shifted(d, j)
         keep_first = jnp.where(jnp.logical_and(d == 1, shift), 0.0, 1.0)
         keep_last = jnp.where(jnp.logical_and(d == depths - 2, shift), 0.0, 1.0)
         slot = jnp.where(own, place(d, 3, k), s)
@@ -422,11 +434,12 @@
 
         @pl.when(way == 0)
         def _():
-            relay_copy(relays_up(d, k), s, k).start()
+            for part in range(2):
+                relay_copy(relays_up(d, k, part), s, k, part).start()
 
         near = jnp.logical_or(way == 1, way == 2)
 
-        @pl.when(jnp.logical_and(near, jnp.logical_not(merges(way, k))))
+        @pl.when(jnp.logical_and(near, jnp.logical_not(jnp.logical_or(handed, merges_any(way, k)))))
         def _():
             image_copy(way, s, k).start()
 
@@ -434,94 +447,113 @@
         late_way, _, late_k = order(d, late)
         due = jnp.logical_and(s - LAG >= per, s - LAG < sent)
 
-        @pl.when(jnp.logical_and(due, merges(late_way, late_k)))
-        def _():
-            merge(late_way, late, late_k)
+        for part in range(2):
+
+            @pl.when(jnp.logical_and(due, merges(late_way, late_k, part)))
+            def _():
+                merge(late_way, late, late_k, part)
+
+        @pl.when(jnp.logical_and(due, merges_any(late_way, late_k)))
+        def _():
             image_copy(late_way, late, late_k).start()
 
-        @pl.when(handed)
-        def _():
-            e_wait(k)
+        return 0
+
+    lax.fori_loop(0, blocks, step, 0)
+
+    @pl.when(outer)
+    def _():
+        def complete(n, _):
+            i = jnp.where(d > 0, n, lax.rem(n + per, per + 1))
+            j = taken(d > 0, i)
+            e_wait(i)
 
             @pl.when(has_prev)
             def _():
-                y_copy(0, k).wait_recv()
+                y_copy(0, i).wait_recv()
 
             @pl.when(has_next)
             def _():
-                y_copy(1, k).wait_recv()
-
+                y_copy(1, i).wait_recv()
+
+            away = n == 0
+            s = jnp.where(d > 0, sent - 1, sent - 2)
+            slot = jnp.where(away, s, place(d, 3, n - 1))
             march_one(f_ref, j, extra_z, image.at[slot], shading, d > 0, rows)
 
+            @pl.when(away)
+            def _():
+                image_copy(jnp.where(d > 0, 2, 1), s, per - 1).start()
+
+            return 0
+
+        lax.fori_loop(0, per + 1, complete, 0)
+
+    def drain(j, _):
+        @pl.when(sends_up(d, j))
+        def _():
+            z_copy(0, j).wait_send()
+
+        @pl.when(sends_down(d, j))
+        def _():
+            z_copy(1, j).wait_send()
+
+        @pl.when(has_next)
+        def _():
+            x_copy(0, j).wait_send()
+
+        @pl.when(has_prev)
+        def _():
+            x_copy(1, j).wait_send()
+
         return 0
 
-    lax.fori_loop(0, blocks, step, 0)
-
-    for k in range(per):
+    lax.fori_loop(0, blocks, drain, 0)
+
+    for k in range(per + 1):
+
+        @pl.when(jnp.logical_not(outer))
+        def _():
+            e_copy(k).wait_send()
+
+        @pl.when(jnp.logical_and(outer, has_next))
+        def _():
+            y_copy(0, k).wait_send()
+
+        @pl.when(jnp.logical_and(outer, has_prev))
+        def _():
+            y_copy(1, k).wait_send()
+
+    def compose(k, _):
         for way in (1, 2):
             pltpu.make_async_remote_copy(
                 src_ref=image.at[0],
                 dst_ref=image.at[place(d, way, k)],
-                send_sem=i_send.at[0],
+                send_sem=i_send.at[0, 0],
                 recv_sem=i_recv.at[way - 1, k],
                 device_id=(up_d, t),
                 device_id_type=MESH,
             ).wait_recv()
-
-        def compose(i, _):
-            at = pl.ds(pl.multiple_of(i * SUB, SUB), SUB)
+        for top in range(0, rows, SUB):
+            at = pl.ds(top, SUB)
             seen = image[sent + k, 3, at, :]
             total = [image[sent + k, c, at, :] for c in range(3)]
             for q in (sent + per + k, sent + 2 * per + k):
                 total = [total[c] + seen * image[q, c, at, :] for c in range(3)]
                 seen = seen * image[q, 3, at, :]
             for c in range(3):
-                out[c, at, k * LANES : (k + 1) * LANES] = total[c]
-            out[3, at, k * LANES : (k + 1) * LANES] = 1.0 - seen
-            return 0
-
-        lax.fori_loop(0, rows // SUB, compose, 0)
-
-    def drain(j, _):
-        @pl.when(sends_up(d, j))
-        def _():
-            z_copy(0, j).wait_send()
-
-        @pl.when(sends_down(d, j))
-        def _():
-            z_copy(1, j).wait_send()
-
-        @pl.when(has_next)
-        def _():
-            x_copy(0, j).wait_send()
-
-        @pl.when(has_prev)
-        def _():
-            x_copy(1, j).wait_send()
-
+                out[c, at, columns(k)] = total[c]
+            out[3, at, columns(k)] = 1.0 - seen
         return 0
 
-    lax.fori_loop(0, blocks, drain, 0)
-
-    def drain_images(s, _):
-        relay_copy(d == 0, s, 0).wait_send()
-        return 0
-
-    lax.fori_loop(0, sent, drain_images, 0)
-
-    for k in range(per):
-
-        @pl.when(jnp.logical_not(outer))
-        def _():
-            e_copy(k).wait_send()
-
-        @pl.when(jnp.logical_and(outer, has_next))
-        def _():
-            y_copy(0, k).wait_send()
-
-        @pl.when(jnp.logical_and(outer, has_prev))
-        def _():
-            y_copy(1, k).wait_send()
+    lax.fori_loop(0, per, compose, 0)
+
+    for s in range(sent):
+        if s < per:
+            for part in range(2):
+                relay_copy(d == 0, s, 0, part).wait_send()
+        else:
+            image_copy(jnp.where(d >= 0, 1, 2), s, 0).wait_send()
 
 
 def on_device(depths, tiles, field, absorb, color, light):
@@ -546,14 +578,14 @@
             dma((blocks,)),
             dma((2, blocks)),
             dma((2, blocks)),
-            dma((per,)),
-            dma((per,)),
+            dma((per + 1,)),
+            dma((per + 1,)),
             dma((2, blocks)),
             dma((2, blocks)),
-            dma((2, per)),
-            dma((2, per)),
-            dma((sent,)),
-            dma((2, per)),
+            dma((2, per + 1)),
+            dma((2, per + 1)),
+            dma((2, sent)),
+            dma((2, per, 2)),
             dma((2, per)),
         ],
         compiler_params=pltpu.CompilerParams(

time: 38.9 us -> 38 us (0.977)
  Pallas kernels: 38 us -> 37.1 us
    pallas_call x1, Pallas kernels: 38 us -> 37.1 us  [on_device(): pl.pallas_call(functools.partial(kernel, depths, tiles, slices, rows, blo...]
where the time goes in v5:
time: 38 us; the launch traced here: 37.9 us
  Pallas kernels  37.1 us (98%)
  local copies, waits for them, and re-layouts  0.8 us (2%)
    pallas_call x1, Pallas kernels, on_device(): pl.pallas_call(functools.partial(kernel, depths, tiles, slices, rows, blo...  37.1 us
    unnamed x1, local copies, waits for them, and re-layouts  0.8 us

profile of v5, /device:TPU:15, one launch (start us, length us, event | category | flops | bytes accessed | tf_op | source)
XLA Modules:
  0.0 37.9 jit_solution(12767543880279298052)
XLA Ops:
  0.0 37.1 %shard_map.46 = f32[4,64,512]{2,1,0:T(8,128)S(1)} custom-call(f32[32,64,2048]{2,1,0:T(8,128)} %field.1, f32[2]{0:T(128)} %absorb_in.1, f32[3,4]{1,0:T(4,128)} %color_in.1, f32[3]{0:T(128)} %light_in.1), custom_call_target="tpu_custom_call" | custom-call | tf_op jit(solution)/shard_map/pallas_call | solution.py:565
  37.1 0.8 %copy.6 = f32[4,64,512]{2,1,0:T(8,128)} copy(f32[4,64,512]{2,1,0:T(8,128)S(1)} %shard_map.46) | data formatting | bytes 1048576

commit v6 on v5

--- a/solution.py
+++ b/solution.py
@@ -159,43 +159,6 @@
     for j in range(blocks):
         load(j).start()
 
-    zeros = jnp.zeros((SUB, LANES), jnp.float32)
-    for edge in (0, blocks + 1):
-
-        def clear(z, _):
-            for row in range(0, rows, SUB):
-                f_ref[edge, z, pl.ds(TOP + row, SUB), :] = zeros
-            return 0
-
-        lax.fori_loop(0, slices + 2 * Z0, clear, 0)
-    for present, z, j0, j1 in (
-        (d == 0, Z0 - 1, 0, blocks),
-        (d == 1, Z0 - 1, 0, per),
-        (d == 1, Z0 - 1, 2 * per - 1, 2 * per),
-        (d == depths - 2, Z0 + slices, sent - 1, blocks),
-        (d == depths - 1, Z0 + slices, 0, blocks),
-    ):
-
-        @pl.when(present)
-        def _():
-            def clear(j, _):
-                for row in range(0, rows, SUB):
-                    f_ref[j + 1, z, pl.ds(TOP + row, SUB), :] = zeros
-                return 0
-
-            lax.fori_loop(j0, j1, clear, 0)
-
-    for present, row in ((has_prev, TOP - SUB), (has_next, TOP + rows)):
-
-        @pl.when(jnp.logical_not(present))
-        def _():
-            def clear(j, _):
-                for z in range(slices + 2 * Z0):
-                    f_ref[j + 1, z, pl.ds(row, SUB), :] = zeros
-                return 0
-
-            lax.fori_loop(0, blocks, clear, 0)
-
     beside = has_prev.astype(jnp.int32) + has_next.astype(jnp.int32)
     pl.semaphore_wait(barrier, 2 + beside)
 
@@ -283,20 +246,31 @@
             device_id_type=MESH,
         )
 
-    def start(s, _):
-        j = block(up_d, s)
+    def fixed_block(me, s):
+        if s < per:
+            off, k = 2, s
+        elif s < sent:
+            off, k = (1, depths - 1)[s % 2], (s - per) // 2
+        else:
+            off, k = 0, s - sent
+        owner = me + off
+        return jnp.where(owner >= depths, owner - depths, owner) * per + k
+
+    def start_depth(s):
+        j = fixed_block(up_d, s)
 
         @pl.when(sends_up(d, j))
         def _():
             z_copy(0, j).start()
 
-        j = block(down_d, s)
-
-        @pl.when(sends_down(d, j))
-        def _():
-            z_copy(1, j).start()
-
-        j = block(d, s)
+        i = fixed_block(down_d, s)
+
+        @pl.when(sends_down(d, i))
+        def _():
+            z_copy(1, i).start()
+
+    def start_rows(s):
+        j = fixed_block(d, s)
 
         @pl.when(has_next)
         def _():
@@ -306,14 +280,53 @@
         def _():
             x_copy(1, j).start()
 
-        return 0
-
-    lax.fori_loop(0, blocks, start, 0)
+    for s in range(blocks):
+        start_depth(s)
+        if s >= 2:
+            start_rows(s - 2)
+    for s in range(blocks - 2, blocks):
+        start_rows(s)
 
     @pl.when(jnp.logical_not(outer))
     def _():
         for k in range(per + 1):
             e_copy(k).start()
+
+    zeros = jnp.zeros((SUB, LANES), jnp.float32)
+    for edge in (0, blocks + 1):
+
+        def clear(i, _):
+            for u in range(6):
+                for row in range(0, rows, SUB):
+                    f_ref[edge, 6 * i + u, pl.ds(TOP + row, SUB), :] = zeros
+            return 0
+
+        lax.fori_loop(0, (slices + 2 * Z0) // 6, clear, 0)
+    for present, z, j0, j1 in (
+        (d == 0, Z0 - 1, 0, blocks),
+        (d == 1, Z0 - 1, 0, per),
+        (d == 1, Z0 - 1, 2 * per - 1, 2 * per),
+        (d == depths - 2, Z0 + slices, sent - 1, blocks),
+        (d == depths - 1, Z0 + slices, 0, blocks),
+    ):
+
+        @pl.when(present)
+        def _():
+            for j in range(j0, j1):
+                for row in range(0, rows, SUB):
+                    f_ref[j + 1, z, pl.ds(TOP + row, SUB), :] = zeros
+
+    for present, row in ((has_prev, TOP - SUB), (has_next, TOP + rows)):
+
+        @pl.when(jnp.logical_not(present))
+        def _():
+            def clear(i, _):
+                for j in range(4):
+                    for z in range(slices + 2 * Z0):
+                        f_ref[4 * i + j + 1, z, pl.ds(row, SUB), :] = zeros
+                return 0
+
+            lax.fori_loop(0, blocks // 4, clear, 0)
 
     for copy in params:
         copy.wait()

time: 38 us -> 38 us (level)
  no operation moved by 1% of the time
where the time goes in v6:
time: 38 us; the launch traced here: 37.9 us
  Pallas kernels  37.1 us (98%)
  local copies, waits for them, and re-layouts  0.8 us (2%)
    pallas_call x1, Pallas kernels, on_device(): pl.pallas_call(functools.partial(kernel, depths, tiles, slices, rows, blo...  37.1 us
    unnamed x1, local copies, waits for them, and re-layouts  0.8 us

profile of v6, /device:TPU:15, one launch (start us, length us, event | category | flops | bytes accessed | tf_op | source)
XLA Modules:
  0.0 37.9 jit_solution(9970941793635537846)
XLA Ops:
  0.0 37.1 %shard_map.46 = f32[4,64,512]{2,1,0:T(8,128)S(1)} custom-call(f32[32,64,2048]{2,1,0:T(8,128)} %field.1, f32[2]{0:T(128)} %absorb_in.1, f32[3,4]{1,0:T(4,128)} %color_in.1, f32[3]{0:T(128)} %light_in.1), custom_call_target="tpu_custom_call" | custom-call | tf_op jit(solution)/shard_map/pallas_call | solution.py:578
  37.1 0.8 %copy.6 = f32[4,64,512]{2,1,0:T(8,128)} copy(f32[4,64,512]{2,1,0:T(8,128)S(1)} %shard_map.46) | data formatting | bytes 1048576

commit v7 on v6

--- a/solution.py
+++ b/solution.py
@@ -15,9 +15,9 @@
 Z0 = 2
 GROUP = 2
 UNROLL = 16
-LAG = 4
+LAG = 3
 SPLIT = 2
-CUT = 48
+CUT = 40
 
 
 class Shading:

time: 38 us -> 37.6 us (0.989)
  Pallas kernels: 37.1 us -> 36.7 us
where the time goes in v7:
time: 37.6 us; the launch traced here: 37.5 us
  Pallas kernels  36.7 us (98%)
  local copies, waits for them, and re-layouts  0.8 us (2%)
    pallas_call x1, Pallas kernels, on_device(): pl.pallas_call(functools.partial(kernel, depths, tiles, slices, rows, blo...  36.7 us
    unnamed x1, local copies, waits for them, and re-layouts  0.8 us

profile of v7, /device:TPU:15, one launch (start us, length us, event | category | flops | bytes accessed | tf_op | source)
XLA Modules:
  0.0 37.5 jit_solution(14773044724544196504)
XLA Ops:
  0.0 36.7 %shard_map.46 = f32[4,64,512]{2,1,0:T(8,128)S(1)} custom-call(f32[32,64,2048]{2,1,0:T(8,128)} %field.1, f32[2]{0:T(128)} %absorb_in.1, f32[3,4]{1,0:T(4,128)} %color_in.1, f32[3]{0:T(128)} %light_in.1), custom_call_target="tpu_custom_call" | custom-call | tf_op jit(solution)/shard_map/pallas_call | solution.py:578
  36.8 0.8 %copy.6 = f32[4,64,512]{2,1,0:T(8,128)} copy(f32[4,64,512]{2,1,0:T(8,128)S(1)} %shard_map.46) | data formatting | bytes 1048576

commit v8 on v7

--- a/solution.py
+++ b/solution.py
@@ -15,7 +15,7 @@
 Z0 = 2
 GROUP = 2
 UNROLL = 16
-LAG = 3
+LAG = 2
 SPLIT = 2
 CUT = 40
 

time: 37.6 us -> 37.6 us (level)
  no operation moved by 1% of the time
where the time goes in v8:
time: 37.6 us; the launch traced here: 37.5 us
  Pallas kernels  36.7 us (98%)
  local copies, waits for them, and re-layouts  0.8 us (2%)
    pallas_call x1, Pallas kernels, on_device(): pl.pallas_call(functools.partial(kernel, depths, tiles, slices, rows, blo...  36.7 us
    unnamed x1, local copies, waits for them, and re-layouts  0.8 us

profile of v8, /device:TPU:15, one launch (start us, length us, event | category | flops | bytes accessed | tf_op | source)
XLA Modules:
  0.0 37.5 jit_solution(5879668731479363175)
XLA Ops:
  0.0 36.7 %shard_map.46 = f32[4,64,512]{2,1,0:T(8,128)S(1)} custom-call(f32[32,64,2048]{2,1,0:T(8,128)} %field.1, f32[2]{0:T(128)} %absorb_in.1, f32[3,4]{1,0:T(4,128)} %color_in.1, f32[3]{0:T(128)} %light_in.1), custom_call_target="tpu_custom_call" | custom-call | tf_op jit(solution)/shard_map/pallas_call | solution.py:578
  36.8 0.8 %copy.6 = f32[4,64,512]{2,1,0:T(8,128)} copy(f32[4,64,512]{2,1,0:T(8,128)S(1)} %shard_map.46) | data formatting | bytes 1048576
